TPU v7x, 128 devices: a whole 4x4x4 slice. The times are simulated.
128 devices in a mesh: tile: 32 (over x_hi, y, z), chan: 4 (over x_lo, core).
Axes of the slice: x: 4 (x_hi: 2, x_lo: 2; x = x_hi * 2 + x_lo), y: 4, z: 4, core: 2. Of those that a mesh axis runs over, the one named last changes fastest.
Arguments:
- video: bfloat16 [128, 384, 16, 128], P('tile', 'chan'), may hold values from -30 to 30
- clip_lengths: int32 [32], replicated, may hold values from 1 to 16, 128 in all
- norm_gain: float32 [384], P('chan'), may hold values from 0.5 to 1.5
- norm_shift: float32 [384], P('chan'), may hold values from -3 to 3
- conv_weight: bfloat16 [3, 3, 3, 384, 384], P(None, None, None, None, 'chan'), may hold values from -0.0625 to 0.0625
- conv_bias: float32 [384], P('chan'), may hold values from -3 to 3
Outputs:
- block_out: bfloat16 [128, 384, 16, 128], P('tile', 'chan')
Inputs may be any that keep to these rules, and one draw needn't show every extreme that they name: `clip_lengths`: the clips fill all 128 frames; the longest has exactly 16 frames.
All inputs are finite; a program needn't handle non-finite values.
Results may differ from a plain program's by a relative error of at most 0.0017.
Values may be sent and summed in bfloat16 or wider, within the bound.
A program may use at most 256 MiB of HBM per device.

v0:
```python
import jax
import jax.numpy as jnp
from jax import lax
from jax.sharding import PartitionSpec as P

GROUPS = 32


def shifted(block, axis, distance):
    devices = range(lax.axis_size(axis))
    route = [(i - distance, i) for i in devices if i - distance in devices]
    return lax.ppermute(block, axis, route)


def on_device(video, clip_lengths, norm_gain, norm_shift, conv_weight, conv_bias):
    hi = lax.Precision.HIGHEST
    frames, chans, rows, cols = video.shape
    groups_here = GROUPS // lax.axis_size("chan")
    per_group = chans // groups_here
    x = video.astype(jnp.float32)
    ends = jnp.cumsum(clip_lengths)
    starts = ends - clip_lengths
    frame = lax.axis_index("tile") * frames + jnp.arange(frames, dtype=jnp.int32)
    inside = (frame[:, None] >= starts[None, :]) & (frame[:, None] < ends[None, :])
    member = inside.astype(jnp.float32)
    start_of = jnp.sum(jnp.where(inside, starts[None, :], 0), axis=1)
    grouped = x.reshape(frames, groups_here, per_group, rows, cols)
    count = clip_lengths.astype(jnp.float32) * float(per_group * rows * cols)
    clip_sum = lax.psum(jnp.dot(member.T, jnp.sum(grouped, axis=(2, 3, 4)), precision=hi), "tile")
    mean_frame = jnp.dot(member, clip_sum / count[:, None], precision=hi)
    centered = grouped - mean_frame[:, :, None, None, None]
    clip_sq = lax.psum(
        jnp.dot(member.T, jnp.sum(centered * centered, axis=(2, 3, 4)), precision=hi), "tile"
    )
    scale_frame = jnp.dot(member, lax.rsqrt(clip_sq / count[:, None] + 1e-06), precision=hi)
    normed = (centered * scale_frame[:, :, None, None, None]).reshape(frames, chans, rows, cols)
    normed = normed * norm_gain[None, :, None, None] + norm_shift[None, :, None, None]
    hidden = jax.nn.silu(normed).astype(jnp.bfloat16)
    full = lax.all_gather(hidden, "chan", axis=1, tiled=True)
    before = shifted(full[frames - 2 :], "tile", 1)
    extended = jnp.concatenate([before, full], axis=0)
    padded = jnp.pad(extended, ((0, 0), (0, 0), (1, 1), (1, 1)))
    conv = jnp.zeros((frames, chans, rows, cols), jnp.float32)
    for tap in range(3):
        valid = frame - (2 - tap) >= start_of
        window = padded[tap : tap + frames]
        window = jnp.where(valid[:, None, None, None], window, jnp.zeros_like(window))
        for row_tap in range(3):
            for cell_tap in range(3):
                part_in = window[:, :, row_tap : row_tap + rows, cell_tap : cell_tap + cols]
                conv = conv + jnp.einsum(
                    "fchw,co->fohw",
                    part_in,
                    conv_weight[tap, row_tap, cell_tap],
                    preferred_element_type=jnp.float32,
                )
    return (x + conv + conv_bias[None, :, None, None]).astype(jnp.bfloat16)


def solution(mesh):
    return jax.shard_map(
        on_device,
        mesh=mesh,
        in_specs=(
            P("tile", "chan", None, None),
            P(),
            P("chan"),
            P("chan"),
            P(None, None, None, None, "chan"),
            P("chan"),
        ),
        out_specs=P("tile", "chan", None, None),
        check_vma=False,
    )
```

profile of v0, /device:TPU:6, one launch (start us, length us, event | category | flops | bytes accessed | tf_op | source)
XLA Modules:
  0.0 589.6 jit_solution(4578367702491092528)
XLA Ops:
  6.5 0.0 all-gather.2.cloned.1.call-start
  6.5 0.8 convert_multiply_fusion
  7.3 1.7 convert_reduce_fusion
  9.0 0.1 reduce_sum.36
  9.1 0.7 copy.14
  9.9 0.1 reduce-window.8
  9.9 0.1 reduce.4
  10.0 0.7 sub.24
  10.7 0.1 reduce_sum.44
  10.8 0.2 select_reduce_fusion
  11.0 0.2 fusion.142
  11.1 96.2 %psum.14 = f32[32,8]{0,1:T(8,128)S(1)} all-reduce(f32[32,8]{0,1:T(8,128)S(1)} %fusion.142), channel_id=1, replica_groups=mesh['tile'=32,'chan'=4] {'tile'}, use_global_device_ids=true, to_apply=%region_4.5 | all-reduce | flops 256 | bytes 2048 | tf_op jit(solution)/shard_map/psum | solution.py:29
  107.4 0.1 fusion.135
  107.5 0.1 sub.25
  107.6 0.1 sub.26
  107.6 2.0 fusion.64
  109.7 0.1 reduce_sum.46
  109.7 0.1 reduce_sum.47
  109.8 0.2 fusion.143
  110.0 88.9 %psum.15 = f32[32,8]{0,1:T(8,128)S(1)} all-reduce(f32[32,8]{0,1:T(8,128)S(1)} %fusion.143), channel_id=1, replica_groups=mesh['tile'=32,'chan'=4] {'tile'}, use_global_device_ids=true, to_apply=%region_7.8 | all-reduce | flops 256 | bytes 2048 | tf_op jit(solution)/shard_map/psum | solution.py:32
  198.9 0.1 fusion.131
  199.0 0.1 mul.42
  199.1 0.1 mul.43
  199.2 0.0 copy-done.1
  199.2 0.0 copy-done.5
  199.2 0.0 copy-done.6
  199.2 3.2 fusion.72
  202.4 0.0 all-gather.2.cloned.1.call-update
  202.5 60.0 %all-gather.2.cloned.1.call-done = bf16[4,384,16,128]{3,1,2,0:T(8,128)(2,1)} async-done(((bf16[4,96,16,128]{3,1,2,0:T(8,128)(2,1)}), bf16[4,384,16,128]{3,1,2,0:T(8,128)(2,1)}) %all-gather.2.cloned.1.call-update) | async-done | bytes 6291472 | tf_op jit(solution)/shard_map/all_gather | solution.py:39
  262.4 2.4 slice.232
  264.8 3.6 collective-permute-start
  268.4 74.9 %collective-permute-done = bf16[2,384,16,128]{3,1,2,0:T(8,128)(2,1)S(1)} collective-permute-done((bf16[2,384,16,128]{3,1,2,0:T(8,128)(2,1)S(1)}, bf16[2,384,16,128]{3,1,2,0:T(8,128)(2,1)S(1)}, u32[]{:S(2)}, u32[]{:S(2)}) %collective-permute-start) | collective-permute-done | bytes 3145760 | tf_op jit(solution)/shard_map/ppermute | solution.py:12
  343.3 0.0 copy-done.2
  343.3 11.0 %fusion.6 = bf16[6,384,18,130]{3,1,2,0:T(8,128)(2,1)} fusion(bf16[4,384,16,128]{3,1,2,0:T(8,128)(2,1)S(1)} %copy-done.2, bf16[2,384,16,128]{3,1,2,0:T(8,128)(2,1)S(1)} %collective-permute-done), kind=kLoop, calls=%fused_computation.10 | loop fusion | flops 80870400 | bytes 20219904 | tf_op jit(solution)/shard_map/concatenate | solution.py:41
  354.3 25.2 %slice_select_fusion.2 = (bf16[4,384,18,130]{3,1,2,0:T(8,128)(2,1)}, bf16[4,384,18,130]{3,1,2,0:T(8,128)(2,1)}, bf16[4,384,18,130]{3,1,2,0:T(8,128)(2,1)S(1)}) fusion(bf16[6,384,18,130]{3,1,2,0:T(8,128)(2,1)} %fusion.6, pred[4]{0:T(512)(128)(4,1)S(1)} %get-tuple-element.10, pred[4]{0:T(512)(128)(4,1)S(1)} %get-tuple-element.12, ...), kind=kLoop, calls=%fused_computation.14 | loop fusion | flops 10782720 | bytes 43130892 | tf_op jit(solution)/shard_map/jit(_where)/select_n | solution.py:47
  379.6 13.6 %fusion.44 = f32[4,16,128,96]{2,3,1,0:T(8,128)} fusion(bf16[4,384,18,130]{3,1,2,0:T(8,128)(2,1)} %get-tuple-element.7, bf16[3,3,3,384,96]{3,4,2,1,0:T(8,128)(2,1)S(1)} %copy-done.3), kind=kOutput, calls=%fused_computation.51 | convolution fusion | flops 603979776 | bytes 9510912 | tf_op jit(solution)/shard_map/fchw,co->fohw/dot_general | solution.py:51
  393.1 8.5 %fusion.46 = f32[4,16,128,96]{2,3,1,0:T(8,128)} fusion(bf16[4,384,18,130]{3,1,2,0:T(8,128)(2,1)} %get-tuple-element.7, bf16[3,3,3,384,96]{3,4,2,1,0:T(8,128)(2,1)S(1)} %copy-done.3), kind=kOutput, calls=%fused_computation.53 | convolution fusion | flops 603979776 | bytes 9510912 | tf_op jit(solution)/shard_map/fchw,co->fohw/dot_general | solution.py:51
  401.6 5.8 fusion.48
  407.4 8.5 %fusion.50 = f32[4,16,128,96]{2,3,1,0:T(8,128)} fusion(bf16[4,384,18,130]{3,1,2,0:T(8,128)(2,1)} %get-tuple-element.7, bf16[3,3,3,384,96]{3,4,2,1,0:T(8,128)(2,1)S(1)} %copy-done.3), kind=kOutput, calls=%fused_computation.57 | convolution fusion | flops 603979776 | bytes 9510912 | tf_op jit(solution)/shard_map/fchw,co->fohw/dot_general | solution.py:51
  415.9 8.5 %fusion.52 = f32[4,16,128,96]{2,3,1,0:T(8,128)} fusion(bf16[4,384,18,130]{3,1,2,0:T(8,128)(2,1)} %get-tuple-element.7, bf16[3,3,3,384,96]{3,4,2,1,0:T(8,128)(2,1)S(1)} %copy-done.3), kind=kOutput, calls=%fused_computation.59 | convolution fusion | flops 603979776 | bytes 9510912 | tf_op jit(solution)/shard_map/fchw,co->fohw/dot_general | solution.py:51
  424.4 5.7 fusion.54
  430.1 8.6 %fusion.56 = f32[4,16,128,96]{2,3,1,0:T(8,128)} fusion(bf16[4,384,18,130]{3,1,2,0:T(8,128)(2,1)} %get-tuple-element.7, bf16[3,3,3,384,96]{3,4,2,1,0:T(8,128)(2,1)S(1)} %copy-done.3), kind=kOutput, calls=%fused_computation.63 | convolution fusion | flops 603979776 | bytes 9510912 | tf_op jit(solution)/shard_map/fchw,co->fohw/dot_general | solution.py:51
  438.7 8.5 %fusion.58 = f32[4,16,128,96]{2,3,1,0:T(8,128)} fusion(bf16[4,384,18,130]{3,1,2,0:T(8,128)(2,1)} %get-tuple-element.7, bf16[3,3,3,384,96]{3,4,2,1,0:T(8,128)(2,1)S(1)} %copy-done.3), kind=kOutput, calls=%fused_computation.65 | convolution fusion | flops 603979776 | bytes 9510912 | tf_op jit(solution)/shard_map/fchw,co->fohw/dot_general | solution.py:51
  447.2 5.7 fusion.60
  453.0 8.4 %fusion.26 = f32[4,16,128,96]{2,3,1,0:T(8,128)} fusion(bf16[4,384,18,130]{3,1,2,0:T(8,128)(2,1)} %get-tuple-element.8, bf16[3,3,3,384,96]{3,4,2,1,0:T(8,128)(2,1)S(1)} %copy-done.3), kind=kOutput, calls=%fused_computation.33 | convolution fusion | flops 603979776 | bytes 9510912 | tf_op jit(solution)/shard_map/fchw,co->fohw/dot_general | solution.py:51
  461.4 8.5 %fusion.28 = f32[4,16,128,96]{2,3,1,0:T(8,128)} fusion(bf16[4,384,18,130]{3,1,2,0:T(8,128)(2,1)} %get-tuple-element.8, bf16[3,3,3,384,96]{3,4,2,1,0:T(8,128)(2,1)S(1)} %copy-done.3), kind=kOutput, calls=%fused_computation.35 | convolution fusion | flops 603979776 | bytes 9510912 | tf_op jit(solution)/shard_map/fchw,co->fohw/dot_general | solution.py:51
  469.9 5.7 fusion.30
  475.6 8.9 %fusion.32 = f32[4,16,128,96]{2,3,1,0:T(8,128)} fusion(bf16[4,384,18,130]{3,1,2,0:T(8,128)(2,1)} %get-tuple-element.8, bf16[3,3,3,384,96]{3,4,2,1,0:T(8,128)(2,1)S(1)} %copy-done.3), kind=kOutput, calls=%fused_computation.39 | convolution fusion | flops 603979776 | bytes 9510912 | tf_op jit(solution)/shard_map/fchw,co->fohw/dot_general | solution.py:51
  484.5 8.4 %fusion.34 = f32[4,16,128,96]{2,3,1,0:T(8,128)} fusion(bf16[4,384,18,130]{3,1,2,0:T(8,128)(2,1)} %get-tuple-element.8, bf16[3,3,3,384,96]{3,4,2,1,0:T(8,128)(2,1)S(1)} %copy-done.3), kind=kOutput, calls=%fused_computation.41 | convolution fusion | flops 603979776 | bytes 9510912 | tf_op jit(solution)/shard_map/fchw,co->fohw/dot_general | solution.py:51
  493.0 5.8 fusion.36
  498.7 8.6 %fusion.38 = f32[4,16,128,96]{2,3,1,0:T(8,128)} fusion(bf16[4,384,18,130]{3,1,2,0:T(8,128)(2,1)} %get-tuple-element.8, bf16[3,3,3,384,96]{3,4,2,1,0:T(8,128)(2,1)S(1)} %copy-done.3), kind=kOutput, calls=%fused_computation.45 | convolution fusion | flops 603979776 | bytes 9510912 | tf_op jit(solution)/shard_map/fchw,co->fohw/dot_general | solution.py:51
  507.3 8.5 %fusion.40 = f32[4,16,128,96]{2,3,1,0:T(8,128)} fusion(bf16[4,384,18,130]{3,1,2,0:T(8,128)(2,1)} %get-tuple-element.8, bf16[3,3,3,384,96]{3,4,2,1,0:T(8,128)(2,1)S(1)} %copy-done.3), kind=kOutput, calls=%fused_computation.47 | convolution fusion | flops 603979776 | bytes 9510912 | tf_op jit(solution)/shard_map/fchw,co->fohw/dot_general | solution.py:51
  515.8 5.8 fusion.42
  521.5 3.9 fusion.10
  525.4 3.2 fusion.12
  528.6 3.9 fusion.14
  532.5 3.9 fusion.16
  536.4 3.0 fusion.18
  539.4 4.0 fusion.20
  543.4 3.9 fusion.22
  547.3 3.0 fusion.24
  550.3 0.0 copy-done.4
  550.3 30.6 %fusion.74 = bf16[4,96,16,128]{3,1,2,0:T(8,128)(2,1)S(1)} fusion(f32[4,16,128,96]{2,3,1,0:T(8,128)} %fusion.10, f32[4,16,128,96]{2,3,1,0:T(8,128)} %fusion.12, f32[4,16,128,96]{2,3,1,0:T(8,128)} %fusion.14, f32[4,16,128,96]{2,3,1,0:T(8,128)} %fusion.16, f32[4,16,128,96]{2,3,1,0:T(8,128)} %fusion.18, f32[4,16,128,96]{2,3,1,0:T(8,128)} %fusion.20, ...), kind=kOutput, calls=%fused_computation.84 | convolution fusion | flops 627572736 | bytes 91300224 | tf_op jit(solution)/shard_map/fchw,co->fohw/dot_general | solution.py:51
  580.8 1.8 copy.15
  (11 shorter events, 0.0 us)
Async XLA Ops:
  6.5 192.7 %copy-start.1 = (bf16[4,96,16,128]{3,2,1,0:T(8,128)(2,1)S(1)}, bf16[4,96,16,128]{3,2,1,0:T(8,128)(2,1)}, u32[]{:S(2)}) copy-start(bf16[4,96,16,128]{3,2,1,0:T(8,128)(2,1)} %param.6) | copy-start | bytes 4718596
  6.5 192.7 %copy-start.5 = (f32[96]{0:T(128)S(1)}, f32[96]{0:T(128)}, u32[]{:S(2)}) copy-start(f32[96]{0:T(128)} %param.9) | copy-start | bytes 1156
  6.5 192.7 %copy-start.6 = (f32[96]{0:T(128)S(1)}, f32[96]{0:T(128)}, u32[]{:S(2)}) copy-start(f32[96]{0:T(128)} %param.8) | copy-start | bytes 1156
  6.5 255.9 %all-gather.2.cloned.1.call-start = ((), (), s32[]{:S(2)}) async-start(), calls=%async_computation | async-start | bytes 7864320 | tf_op jit(solution)/shard_map/all_gather | solution.py:39
  262.4 80.9 %copy-start.2 = (bf16[4,384,16,128]{3,1,2,0:T(8,128)(2,1)S(1)}, bf16[4,384,16,128]{3,1,2,0:T(8,128)(2,1)}, u32[]{:S(2)}) copy-start(bf16[4,384,16,128]{3,1,2,0:T(8,128)(2,1)} %all-gather.2.cloned.1.call-done) | copy-start | bytes 18874372
  264.8 78.5 %collective-permute-start = (bf16[2,384,16,128]{3,1,2,0:T(8,128)(2,1)S(1)}, bf16[2,384,16,128]{3,1,2,0:T(8,128)(2,1)S(1)}, u32[]{:S(2)}, u32[]{:S(2)}) collective-permute-start(bf16[2,384,16,128]{3,1,2,0:T(8,128)(2,1)S(1)} %slice.232), channel_id=1, source_target_pairs={{0,4},{4,8},{8,12},{12,16},{16,20},{20,24},{24,28},{28,32},{32,36}... | collective-permute-start | bytes 9437192 | tf_op jit(solution)/shard_map/ppermute | solution.py:12
  354.3 25.2 %copy-start.3 = (bf16[3,3,3,384,96]{3,4,2,1,0:T(8,128)(2,1)S(1)}, bf16[3,3,3,384,96]{3,4,2,1,0:T(8,128)(2,1)}, u32[]{:S(2)}) copy-start(bf16[3,3,3,384,96]{3,4,2,1,0:T(8,128)(2,1)} %param.10) | copy-start | bytes 5971972
  379.5 167.8 %copy-start = (bf16[4,384,18,130]{3,1,2,0:T(8,128)(2,1)}, bf16[4,384,18,130]{3,1,2,0:T(8,128)(2,1)S(1)}, u32[]{:S(2)}) copy-start(bf16[4,384,18,130]{3,1,2,0:T(8,128)(2,1)S(1)} %get-tuple-element.9) | copy-start | bytes 21565444
  547.3 3.0 copy-start.4
Sparse Core Ops, SparseCore 0:
  202.6 59.7 all-gather.1
where the time goes:
time: 595 us; the launch traced here: 590 us
  matrix products  202 us (34%)
  blocking collectives  185 us (31%)
  waiting for transfers between devices  135 us (23%)
  other arithmetic  45.1 us (8%)
  between operations  13.7 us (2%)
    dot_general x27, matrix products, on_device(): jnp.einsum('fchw,co->fohw', part_in, conv_weight[tap, row_tap, cell_tap],...  201 us
    psum x1, blocking collectives, on_device(): lax.psum(jnp.dot(member.T, jnp.sum(grouped, axis=(2, 3, 4)), precision=hi...  96.2 us
    psum x1, blocking collectives, on_device(): lax.psum(jnp.dot(member.T, jnp.sum(centered * centered, axis=(2, 3, 4)),...  88.9 us
    ppermute x1, waiting for transfers between devices, shifted(): return lax.ppermute(block, axis, route)  74.9 us
    all_gather x1, waiting for transfers between devices, on_device(): full = lax.all_gather(hidden, 'chan', axis=1, tiled=True)  60 us
    select_n x1, other arithmetic, on_device(): jnp.where(valid[:, None, None, None], window, jnp.zeros_like(window))  25.2 us
  transfers between devices with their start and end apart: 2, of which 2 were waited for; matrix products, arithmetic and copies ran while one was open for 0% of the time, Pallas kernels for 0%

commit v1 on v0

v1 whole, which is shorter than its diff:
```python
import jax
import jax.numpy as jnp
from jax import lax
from jax.experimental import pallas as pl
from jax.experimental.pallas import tpu as pltpu
from jax.sharding import PartitionSpec as P

MESH = pl.DeviceIdType.MESH
F32 = jnp.float32
BF16 = jnp.bfloat16
PER_GROUP = 12
HOPS = (1, -1, 2, -2, 3, -3, 4, -4)
EPS = 1e-06


def swap_matrix():
    row = lax.broadcasted_iota(jnp.int32, (256, 256), 0)
    col = lax.broadcasted_iota(jnp.int32, (256, 256), 1)
    return jnp.where(col == (row % 16) * 16 + row // 16, 1.0, 0.0).astype(BF16)


def kernel(
    lens, gain, shift, bias, video, weight, out,
    raw_own, raw_sib, raw_x, raw_xs, slab, wt, hid_a, hid_b, acc, pout, pin, obuf, ab, abmsg, par, swap, srow, mrow, stat, msk,
    own_sem, w_sem, out_sem, xs, xr, ss, sr, fs, fr, ts, tr, cs, cr, ps, pr,
):
    frames, chans, rows, cols = video.shape
    groups = chans // PER_GROUP
    half = chans // 2
    kdim = 9 * 2 * chans
    row_k = 3 * 2 * chans
    t, c = lax.axis_index("tile"), lax.axis_index("chan")
    tiles = lax.axis_size("tile")

    def tile_at(hop):
        return (lax.rem(t + hop + tiles, tiles), c)

    def mate(r):
        return (t, c + r - 2 * (c % 2) if r == 1 else c + 2 - 4 * (c // 2) if r == 2 else 3 - c)

    def remote(src, dst, send, recv, dev):
        return pltpu.make_async_remote_copy(
            src_ref=src, dst_ref=dst, send_sem=send, recv_sem=recv, device_id=dev, device_id_type=MESH
        )

    def half_frame(k):
        return pl.ds((k % 2) * half, half)

    def to_x(k):
        f, here = k // 2, half_frame(k)
        return remote(video.at[f, here], raw_x.at[f, here], xs.at[k], xr.at[k], mate(2))

    def to_sibling(f):
        return remote(video.at[f], raw_sib.at[f], ss.at[f], sr.at[f], mate(1))

    def forward(k):
        f, here = k // 2, half_frame(k)
        return remote(raw_x.at[f, here], raw_xs.at[f, here], fs.at[k], fr.at[k], mate(1))

    def send_stat(i):
        return remote(stat.at[8], stat.at[i], ts.at[i], tr.at[i], tile_at(HOPS[i]))

    def send_ab(r):
        return remote(abmsg.at[0], abmsg.at[r], cs.at[r], cr.at[r], mate(r))

    def send_part(i):
        return remote(pout.at[i], pin.at[i], ps.at[i], pr.at[i], (lax.rem(t + 1, tiles), c))

    def own_copy(f):
        return pltpu.make_async_copy(video.at[f], raw_own.at[f], own_sem.at[f])

    def out_copy(f):
        return pltpu.make_async_copy(obuf.at[f], out.at[f], out_sem.at[f])

    def w_copy(dt):
        return pltpu.make_async_copy(weight.at[dt], slab.at[dt], w_sem.at[dt])

    for f in range(frames):
        own_copy(f).start()
    barrier = pltpu.get_barrier_semaphore()
    neighbours = [tile_at(h) for h in HOPS] + [mate(r) for r in (1, 2, 3)]
    for d in neighbours:
        pl.semaphore_signal(barrier, inc=1, device_id=d, device_id_type=MESH)
    pl.semaphore_wait(barrier, len(neighbours))
    order = [2 * f + j for f in reversed(range(frames)) for j in range(2)]
    for k in order[:3]:
        to_x(k).start()
    for f in reversed(range(frames)):
        to_sibling(f).start()
    for dt in range(3):
        w_copy(dt).start()

    for f in range(frames):
        own_copy(f).wait()
    count = float(PER_GROUP * rows * cols)

    def sums(i, _):
        x = raw_own[i // groups, pl.ds((i % groups) * PER_GROUP, PER_GROUP)].astype(F32)
        srow[pl.ds(i, 1), :] = jnp.sum(jnp.sum(x, axis=0), axis=0, keepdims=True)
        return _

    lax.fori_loop(0, frames * groups, sums, 0)
    mrow[...] = jnp.broadcast_to(jnp.sum(srow[...], axis=1, keepdims=True) / count, mrow.shape)

    def squares(i, _):
        x = raw_own[i // groups, pl.ds((i % groups) * PER_GROUP, PER_GROUP)].astype(F32)
        d = x - mrow[pl.ds(i, 1), :][None]
        srow[pl.ds(i, 1), :] = jnp.sum(jnp.sum(d * d, axis=0), axis=0, keepdims=True)
        return _

    lax.fori_loop(0, frames * groups, squares, 0)
    sq = jnp.broadcast_to(jnp.sum(srow[...], axis=1, keepdims=True), srow.shape)
    lane = lax.broadcasted_iota(jnp.int32, (groups, cols), 1)
    message = jnp.zeros((groups, cols), F32)
    for f in range(frames):
        here = slice(f * groups, (f + 1) * groups)
        message = jnp.where(lane // 16 == f, mrow[here, :], message)
        message = jnp.where(lane // 16 == frames + f, sq[here], message)
    stat[8] = message
    for i, hop in enumerate(HOPS):

        @pl.when((t + hop >= 0) & (t + hop < tiles))
        def _():
            send_stat(i).start()


    first = t * frames

    def bounds(k, carry):
        end, starts, ends = carry
        end = end + lens[k]
        starts = tuple(jnp.where(end <= first + f, end, starts[f]) for f in range(frames))
        ends = tuple(jnp.where(end > first + f, jnp.minimum(ends[f], end), ends[f]) for f in range(frames))
        return end, starts, ends

    zero = jnp.int32(0)
    _, starts, ends = lax.fori_loop(
        0, lens.shape[0], bounds, (zero, (zero,) * frames, (jnp.int32(1 << 20),) * frames)
    )
    for f in range(frames):
        for dt in range(3):
            msk[f * 3 + dt] = jnp.where(first + f + 2 - dt < ends[f], 1.0, 0.0).astype(F32)

    def spread_rows(k, _):
        par[0, pl.ds(k, 1), :] = jnp.full((1, cols), gain[k], F32)
        par[1, pl.ds(k, 1), :] = jnp.full((1, cols), shift[k], F32)
        par[2, pl.ds(k, 1), :] = jnp.full((1, cols), bias[k], F32)
        return _

    lax.fori_loop(0, chans, spread_rows, 0)
    swap[...] = swap_matrix()

    for part in range(2):
        acc[frames + part] = jnp.zeros((rows, chans, cols), F32)

    def tiles_of(ref, at):
        return jnp.concatenate([ref[(*at, pl.ds(16 * j, 16))].reshape(256, cols) for j in range(chans // 16)], axis=1)

    def begin(f, _):
        y = jnp.dot(swap[...], tiles_of(raw_own, (f,)), preferred_element_type=F32)
        for j in range(chans // 16):
            here = slice(16 * j, 16 * (j + 1))
            acc[f, :, here, :] = y[:, j * cols : (j + 1) * cols].reshape(rows, 16, cols) + par[2, here, :][None]
        return _

    lax.fori_loop(0, frames, begin, 0)

    for dt in range(3):
        w_copy(dt).wait()
        for q in range(2):
            for tap in range(9):
                wt[q, dt * chans : (dt + 1) * chans, tap * 2 * chans : (tap + 1) * 2 * chans] = slab[
                    dt, tap, :, q * 2 * chans : (q + 1) * 2 * chans
                ]

    for hid in (hid_a, hid_b):
        hid[0:row_k, :] = jnp.zeros((row_k, cols), BF16)
        hid[17 * row_k : 18 * row_k, :] = jnp.zeros((row_k, cols), BF16)

    for i, hop in enumerate(HOPS):

        @pl.when((t - hop >= 0) & (t - hop < tiles))
        def _():
            send_stat(i).wait_recv()

    lane_frame = (lane // 16) % frames
    is_mean = lane // 16 < frames
    scales = jnp.zeros((chans, cols), F32)
    lane_c = lax.broadcasted_iota(jnp.int32, (chans, cols), 1)
    row8 = lax.broadcasted_iota(jnp.int32, (8, cols), 0)

    def per_channel(v):
        blocks = []
        for b in range(chans // 8):
            g0, g1 = (8 * b) // PER_GROUP, (8 * b + 7) // PER_GROUP
            lo = jnp.broadcast_to(v[g0 : g0 + 1], (8, cols))
            if g1 != g0:
                lo = jnp.where(row8 < (g0 + 1) * PER_GROUP - 8 * b, lo, jnp.broadcast_to(v[g1 : g1 + 1], (8, cols)))
            blocks.append(lo)
        return jnp.concatenate(blocks, axis=0)

    hops = (*HOPS, 0)
    for f in range(frames):
        inside = []
        for h in hops:
            at = (t - h) * frames + lane_frame
            inside.append((at >= starts[f]) & (at < ends[f]))
        length = (ends[f] - starts[f]).astype(F32)
        total = jnp.zeros((groups, cols), F32)
        for i in range(9):
            total = total + jnp.where(inside[i] & is_mean, stat[i], 0.0)
        mean = jnp.sum(total, axis=1, keepdims=True) / (16.0 * length)
        total = jnp.zeros((groups, cols), F32)
        for i in range(9):
            d = stat[i] - mean
            total = total + jnp.where(inside[i], jnp.where(is_mean, d * d, stat[i] * (1.0 / count)), 0.0)
        spread = jnp.sum(total, axis=1, keepdims=True) / (16.0 * length)
        rstd = lax.rsqrt(spread + EPS)
        a = 0.5 * (per_channel(jnp.broadcast_to(rstd, (groups, cols))) * par[0])
        b = 0.5 * par[1] - per_channel(jnp.broadcast_to(mean, (groups, cols))) * a
        ab[0, 0, f] = a
        ab[0, 1, f] = b
        scales = jnp.where(lane_c // 16 == f, a, scales)
        scales = jnp.where(lane_c // 16 == frames + f, b, scales)
    abmsg[0] = scales
    for r in (2, 3, 1):
        send_ab(r).start()
    for k in order[3:]:
        to_x(k).start()

    def expand(r):
        for f in range(frames):
            ab[r, 0, f] = jnp.broadcast_to(abmsg[r, :, 16 * f : 16 * f + 1], (chans, cols))
            lo = 16 * (frames + f)
            ab[r, 1, f] = jnp.broadcast_to(abmsg[r, :, lo : lo + 1], (chans, cols))

    lane_t = lax.broadcasted_iota(jnp.int32, (16, cols), 1)

    def normalize(slot, f, hid, place):
        y = jnp.dot(swap[...], tiles_of((raw_own, raw_sib, raw_x, raw_xs)[slot], (f,)), preferred_element_type=F32)
        for j in range(chans // 16):
            here = slice(16 * j, 16 * (j + 1))
            a, b = ab[slot, 0, f, here, :], ab[slot, 1, f, here, :]
            for h in range(rows):
                z = y[h * 16 : (h + 1) * 16, j * cols : (j + 1) * cols] * a + b
                z = z + z * jnp.tanh(z)
                left = jnp.where(lane_t == 0, 0.0, pltpu.roll(z, 1, 1))
                right = jnp.where(lane_t == cols - 1, 0.0, pltpu.roll(z, cols - 1, 1))
                for dw, piece in enumerate((left, z, right)):
                    to = pl.multiple_of(((h + 1) * 3 + dw) * 2 * chans + place * chans + 16 * j, 16)
                    hid[pl.ds(to, 16), :] = piece.astype(BF16)

    def convolve(q, f, hid, first_row, n):
        pieces = [hid[pl.ds(pl.multiple_of((first_row + j) * row_k, row_k), kdim), :] for j in range(n)]
        res = jnp.dot(wt[q], jnp.concatenate(pieces, axis=1), preferred_element_type=F32)
        for dt in range(3):
            m = msk[f * 3 + dt]
            for j in range(n):
                part = res[dt * chans : (dt + 1) * chans, j * cols : (j + 1) * cols]
                acc[f + 2 - dt, first_row + j] += part * m

    def stage(conv, norm):
        n = rows // 2

        for p in range(2):
            if conv is not None:
                q, f = conv
                convolve(q + (1 - 2 * q) * (c // 2), f, hid_of[conv], p * n, n)
            if norm is not None:
                q, f = norm
                normalize(2 * q + p, f, hid_of[norm], p + (1 - 2 * p) * (c % 2))

    def finish(f):
        pieces = []
        for j in range(chans // 16):
            here = slice(16 * j, 16 * (j + 1))
            value = acc[f, :, here, :]
            pieces.append(value.astype(BF16).reshape(256, cols))
        y = jnp.dot(swap[...], jnp.concatenate(pieces, axis=1), preferred_element_type=F32).astype(BF16)
        for j in range(chans // 16):
            obuf[f, 16 * j : 16 * (j + 1)] = y[:, j * cols : (j + 1) * cols].reshape(16, rows, cols)
        out_copy(f).start()

    def arrived(f):
        for k in (2 * f, 2 * f + 1):
            to_x(k).wait_recv()
            forward(k).start()

    def forwarded(f):
        for k in (2 * f, 2 * f + 1):
            forward(k).wait_recv()

    def send_halo(i):
        @pl.when(t < tiles - 1)
        def _():
            pout[i] = acc[frames + i].astype(BF16)
            send_part(i).start()

    own, rem = 0, 1
    steps = [(own, 3), (own, 2), (rem, 3), (own, 1), (rem, 2), (own, 0), (rem, 1), (rem, 0)]
    hid_of = {step: (hid_a, hid_b)[i % 2] for i, step in enumerate(steps)}

    send_ab(1).wait_recv()
    expand(1)
    for f in range(frames):
        to_sibling(f).wait_recv()
    with jax.named_scope("norm_first"):
        stage(None, (own, 3))
    with jax.named_scope("own3"):
        stage((own, 3), (own, 2))
    arrived(3)
    send_ab(2).wait_recv()
    expand(2)
    send_ab(3).wait_recv()
    expand(3)
    forwarded(3)
    with jax.named_scope("own2"):
        stage((own, 2), (rem, 3))
    with jax.named_scope("rem3"):
        stage((rem, 3), (own, 1))
    send_halo(1)
    with jax.named_scope("wait2"):
        arrived(2)
        forwarded(2)
    with jax.named_scope("own1"):
        stage((own, 1), (rem, 2))
    with jax.named_scope("rem2"):
        stage((rem, 2), (own, 0))
    send_halo(0)
    with jax.named_scope("wait1"):
        arrived(1)
        forwarded(1)
    with jax.named_scope("own0"):
        stage((own, 0), (rem, 1))
    with jax.named_scope("rem1"):
        stage((rem, 1), None)
    finish(3)
    with jax.named_scope("wait0"):
        arrived(0)
        forwarded(0)
    with jax.named_scope("norm_last"):
        stage(None, (rem, 0))
    with jax.named_scope("rem0"):
        stage((rem, 0), None)
    with jax.named_scope("finish"):
        finish(2)
        for i in range(2):

            @pl.when(t > 0)
            def _():
                send_part(1 - i).wait_recv()
                acc[1 - i] += pin[1 - i].astype(F32)

            finish(1 - i)

    for i in range(2):

        @pl.when(t < tiles - 1)
        def _():
            send_part(i).wait_send()

    for f in range(frames):
        out_copy(f).wait()
        to_sibling(f).wait_send()
    for k in order:
        to_x(k).wait_send()
        forward(k).wait_send()
    for i, hop in enumerate(HOPS):

        @pl.when((t + hop >= 0) & (t + hop < tiles))
        def _():
            send_stat(i).wait_send()

    for r in (1, 2, 3):
        send_ab(r).wait_send()


def on_device(video, clip_lengths, norm_gain, norm_shift, conv_weight, conv_bias):
    frames, chans, rows, cols = video.shape
    groups = chans // PER_GROUP
    all_chans = conv_weight.shape[3]
    weight = jnp.swapaxes(conv_weight, 3, 4).reshape(3, 9, chans, all_chans)
    dma = pltpu.SemaphoreType.DMA
    smem, anyspace = pl.BlockSpec(memory_space=pltpu.SMEM), pl.BlockSpec(memory_space=pl.ANY)
    return pl.pallas_call(
        kernel,
        out_shape=jax.ShapeDtypeStruct(video.shape, BF16),
        in_specs=[smem] * 4 + [anyspace] * 2,
        out_specs=anyspace,
        scratch_shapes=[
            pltpu.VMEM((frames, chans, rows, cols), BF16),
            pltpu.VMEM((frames, chans, rows, cols), BF16),
            pltpu.VMEM((frames, chans, rows, cols), BF16),
            pltpu.VMEM((frames, chans, rows, cols), BF16),
            pltpu.VMEM((3, 9, chans, 4 * chans), BF16),
            pltpu.VMEM((2, 3 * chans, 18 * chans), BF16),
            pltpu.VMEM((18 * 6 * chans, cols), BF16),
            pltpu.VMEM((18 * 6 * chans, cols), BF16),
            pltpu.VMEM((frames + 2, rows, chans, cols), F32),
            pltpu.VMEM((2, rows, chans, cols), BF16),
            pltpu.VMEM((2, rows, chans, cols), BF16),
            pltpu.VMEM((frames, chans, rows, cols), BF16),
            pltpu.VMEM((4, 2, frames, chans, cols), F32),
            pltpu.VMEM((4, chans, cols), F32),
            pltpu.VMEM((3, chans, cols), F32),
            pltpu.VMEM((256, 256), BF16),
            pltpu.VMEM((frames * groups, cols), F32),
            pltpu.VMEM((frames * groups, cols), F32),
            pltpu.VMEM((9, groups, cols), F32),
            pltpu.SMEM((3 * frames,), F32),
            dma((frames,)), dma((3,)), dma((frames,)),
            dma((2 * frames,)), dma((2 * frames,)), dma((frames,)), dma((frames,)), dma((2 * frames,)), dma((2 * frames,)),
            dma((8,)), dma((8,)), dma((4,)), dma((4,)), dma((2,)), dma((2,)),
        ],
        compiler_params=pltpu.CompilerParams(
            collective_id=0, has_side_effects=True, vmem_limit_bytes=60 << 20
        ),
        name="resblock",
    )(clip_lengths, norm_gain, norm_shift, conv_bias, video, weight)


def solution(mesh):
    return jax.shard_map(
        on_device,
        mesh=mesh,
        in_specs=(
            P("tile", "chan", None, None),
            P(),
            P("chan"),
            P("chan"),
            P(None, None, None, None, "chan"),
            P("chan"),
        ),
        out_specs=P("tile", "chan", None, None),
        check_vma=False,
    )
```

time: 595 us -> 74.1 us (0.12)
  matrix products: 202 us -> 0 us
  blocking collectives: 185 us -> 0 us
  waiting for transfers between devices: 135 us -> 0 us
  Pallas kernels: 0 us -> 71.1 us
  other arithmetic: 45.1 us -> 0 us
  between operations: 13.7 us -> 0.01 us
    dot_general x31 -> x0, matrix products: 202 us -> none  [the longest x27 201 us: on_device(): jnp.einsum('fchw,co->fohw', part_in, conv_weight[tap, row_tap, cell_tap],...]
    psum x2 -> x0, blocking collectives: 185 us -> none  [the longest x1 96.2 us: on_device(): lax.psum(jnp.dot(member.T, jnp.sum(grouped, axis=(2, 3, 4)), precision=hi...]
    ppermute x1 -> x0, waiting for transfers between devices: 74.9 us -> none  [shifted(): return lax.ppermute(block, axis, route)]
    pallas_call x0 -> x1, Pallas kernels: none -> 71.1 us  [on_device(): pl.pallas_call(kernel, out_shape=jax.ShapeDtypeStruct(video.shape, BF16),...]
    all_gather x1 -> x0, waiting for transfers between devices: 60 us -> none  [on_device(): full = lax.all_gather(hidden, 'chan', axis=1, tiled=True)]
    select_n x1 -> x0, other arithmetic: 25.2 us -> none  [on_device(): jnp.where(valid[:, None, None, None], window, jnp.zeros_like(window))]
    concatenate x1 -> x0, other arithmetic: 11 us -> none  [on_device(): extended = jnp.concatenate([before, full], axis=0)]
  transfers between devices with their start and end apart: 2 -> 0, of which waited for: 2 -> 0; matrix products, arithmetic and copies ran while one was open for 0% -> 0% of each run, Pallas kernels for 0% -> 0%
where the time goes in v1:
time: 74.1 us; the launch traced here: 74 us
  Pallas kernels  71.1 us (96%)
  local copies, waits for them, and re-layouts  2.82 us (4%)
    pallas_call x1, Pallas kernels, on_device(): pl.pallas_call(kernel, out_shape=jax.ShapeDtypeStruct(video.shape, BF16),...  71.1 us
    unnamed x1, local copies, waits for them, and re-layouts  2.82 us

profile of v1, /device:TPU:6, one launch (start us, length us, event | category | flops | bytes accessed | tf_op | source)
XLA Modules:
  0.0 74.0 jit_solution(3471808910647544904)
XLA Ops:
  0.0 71.1 %resblock.1 = bf16[4,96,16,128]{3,2,1,0:T(8,128)(2,1)} custom-call(s32[32]{0:T(128)} %lens.1, f32[96]{0:T(128)} %gain.1, f32[96]{0:T(128)} %shift.1, f32[96]{0:T(128)} %bias.1, bf16[4,96,16,128]{3,2,1,0:T(8,128)(2,1)} %video.1, bf16[3,9,96,384]{3,2,1,0:T(8,128)(2,1)} %bitcast.3), custom_call_target="tpu_custom_call" | custom-call | tf_op jit(solution)/shard_map/resblock/pallas_call | solution.py:385
  71.1 2.8 %copy.8 = bf16[4,96,16,128]{3,2,1,0:T(8,128)(2,1)} copy(bf16[4,96,16,128]{3,2,1,0:T(8,128)(2,1)} %resblock.1) | data formatting | bytes 3145728

commit v2 on v1

--- a/solution.py
+++ b/solution.py
@@ -11,6 +11,7 @@
 PER_GROUP = 12
 HOPS = (1, -1, 2, -2, 3, -3, 4, -4)
 EPS = 1e-06
+RELAYS = 8
 
 
 def swap_matrix():
@@ -20,9 +21,9 @@
 
 
 def kernel(
-    lens, gain, shift, bias, video, weight, out,
-    raw_own, raw_sib, raw_x, raw_xs, slab, wt, hid_a, hid_b, acc, pout, pin, obuf, ab, abmsg, par, swap, srow, mrow, stat, msk,
-    own_sem, w_sem, out_sem, xs, xr, ss, sr, fs, fr, ts, tr, cs, cr, ps, pr,
+    lens_in, gain_in, shift_in, bias_in, video, weight, out,
+    raw_own, raw_sib, raw_x, raw_xs, slab, wt, hid_a, hid_b, acc, pout, pin, hop_buf, ab, abmsg, par, swap, srow, mrow, stat, msk, lens, gain, shift, bias, par_sem,
+    own_sem, w_sem, xs, xr, ss, sr, fs, fr, ts, tr, cs, cr, ps, pr, hs, hr, qs, qr,
 ):
     frames, chans, rows, cols = video.shape
     groups = chans // PER_GROUP
@@ -66,24 +67,62 @@
     def send_part(i):
         return remote(pout.at[i], pin.at[i], ps.at[i], pr.at[i], (lax.rem(t + 1, tiles), c))
 
+    cross = tiles // 2 - 1
+    first_relay = cross - 10
+    from_first = t - first_relay
+    is_relay = (from_first >= 0) & (from_first < 10) & ((from_first + tiles) % 4 < 3)
+    my_share = from_first - from_first // 4
+    share = rows // RELAYS
+
+    def relay(j):
+        return (first_relay + 4 * (j // 3) + j % 3, c)
+
+    def to_relay(i, j):
+        src = pout.at[i, pl.ds(j * share, share)]
+        return remote(src, hop_buf.at[i], hs.at[i, j], hr.at[i], relay(j))
+
+    def from_relay(i, j):
+        dst = pin.at[i, pl.ds(j * share, share)]
+        return remote(hop_buf.at[i], dst, qs.at[i], qr.at[i, j], (cross + 1, c))
+
     def own_copy(f):
         return pltpu.make_async_copy(video.at[f], raw_own.at[f], own_sem.at[f])
 
-    def out_copy(f):
-        return pltpu.make_async_copy(obuf.at[f], out.at[f], out_sem.at[f])
-
     def w_copy(dt):
         return pltpu.make_async_copy(weight.at[dt], slab.at[dt], w_sem.at[dt])
 
+    small = [
+        pltpu.make_async_copy(src, dst, par_sem.at[i])
+        for i, (src, dst) in enumerate(((lens_in, lens), (gain_in, gain), (shift_in, shift), (bias_in, bias)))
+    ]
     for f in range(frames):
         own_copy(f).start()
+    for copy in small:
+        copy.start()
     barrier = pltpu.get_barrier_semaphore()
-    neighbours = [tile_at(h) for h in HOPS] + [mate(r) for r in (1, 2, 3)]
-    for d in neighbours:
-        pl.semaphore_signal(barrier, inc=1, device_id=d, device_id_type=MESH)
-    pl.semaphore_wait(barrier, len(neighbours))
+    for r in (2, 1, 3):
+        pl.semaphore_signal(barrier, inc=1, device_id=mate(r), device_id_type=MESH)
+    for hop in HOPS:
+
+        @pl.when((t + hop >= 0) & (t + hop < tiles))
+        def _():
+            pl.semaphore_signal(barrier, inc=1, device_id=tile_at(hop), device_id_type=MESH)
+
+    @pl.when((t == cross) | (t == cross + 1))
+    def _():
+        for j in range(RELAYS):
+            pl.semaphore_signal(barrier, inc=1, device_id=relay(j), device_id_type=MESH)
+
+    @pl.when(is_relay)
+    def _():
+        for d in (cross, cross + 1):
+            pl.semaphore_signal(barrier, inc=1, device_id=(d, c), device_id_type=MESH)
+
+    peers = 3 + jnp.minimum(t, 4) + jnp.minimum(tiles - 1 - t, 4)
+    peers = peers + jnp.where((t == cross) | (t == cross + 1), RELAYS, 0) + jnp.where(is_relay, 2, 0)
+    pl.semaphore_wait(barrier, peers)
     order = [2 * f + j for f in reversed(range(frames)) for j in range(2)]
-    for k in order[:3]:
+    for k in order[:1]:
         to_x(k).start()
     for f in reversed(range(frames)):
         to_sibling(f).start()
@@ -94,21 +133,23 @@
         own_copy(f).wait()
     count = float(PER_GROUP * rows * cols)
 
-    def sums(i, _):
-        x = raw_own[i // groups, pl.ds((i % groups) * PER_GROUP, PER_GROUP)].astype(F32)
-        srow[pl.ds(i, 1), :] = jnp.sum(jnp.sum(x, axis=0), axis=0, keepdims=True)
+    def sums(f, _):
+        for g in range(groups):
+            x = raw_own[f, g * PER_GROUP : (g + 1) * PER_GROUP].astype(F32)
+            srow[pl.ds(f * groups + g, 1), :] = jnp.sum(jnp.sum(x, axis=0), axis=0, keepdims=True)
         return _
 
-    lax.fori_loop(0, frames * groups, sums, 0)
+    lax.fori_loop(0, frames, sums, 0)
     mrow[...] = jnp.broadcast_to(jnp.sum(srow[...], axis=1, keepdims=True) / count, mrow.shape)
 
-    def squares(i, _):
-        x = raw_own[i // groups, pl.ds((i % groups) * PER_GROUP, PER_GROUP)].astype(F32)
-        d = x - mrow[pl.ds(i, 1), :][None]
-        srow[pl.ds(i, 1), :] = jnp.sum(jnp.sum(d * d, axis=0), axis=0, keepdims=True)
+    def squares(f, _):
+        for g in range(groups):
+            x = raw_own[f, g * PER_GROUP : (g + 1) * PER_GROUP].astype(F32)
+            d = x - mrow[pl.ds(f * groups + g, 1), :][None]
+            srow[pl.ds(f * groups + g, 1), :] = jnp.sum(jnp.sum(d * d, axis=0), axis=0, keepdims=True)
         return _
 
-    lax.fori_loop(0, frames * groups, squares, 0)
+    lax.fori_loop(0, frames, squares, 0)
     sq = jnp.broadcast_to(jnp.sum(srow[...], axis=1, keepdims=True), srow.shape)
     lane = lax.broadcasted_iota(jnp.int32, (groups, cols), 1)
     message = jnp.zeros((groups, cols), F32)
@@ -123,6 +164,12 @@
         def _():
             send_stat(i).start()
 
+    for k in order[1:3]:
+        to_x(k).start()
+
+
+    for copy in small:
+        copy.wait()
 
     first = t * frames
 
@@ -153,8 +200,10 @@
     for part in range(2):
         acc[frames + part] = jnp.zeros((rows, chans, cols), F32)
 
-    def tiles_of(ref, at):
-        return jnp.concatenate([ref[(*at, pl.ds(16 * j, 16))].reshape(256, cols) for j in range(chans // 16)], axis=1)
+    all_runs = tuple(range(chans // 16))
+
+    def tiles_of(ref, at, runs=all_runs):
+        return jnp.concatenate([ref[(*at, pl.ds(16 * j, 16))].reshape(256, cols) for j in runs], axis=1)
 
     def begin(f, _):
         y = jnp.dot(swap[...], tiles_of(raw_own, (f,)), preferred_element_type=F32)
@@ -225,7 +274,7 @@
     abmsg[0] = scales
     for r in (2, 3, 1):
         send_ab(r).start()
-    for k in order[3:]:
+    for k in order[3:6]:
         to_x(k).start()
 
     def expand(r):
@@ -236,13 +285,15 @@
 
     lane_t = lax.broadcasted_iota(jnp.int32, (16, cols), 1)
 
-    def normalize(slot, f, hid, place):
-        y = jnp.dot(swap[...], tiles_of((raw_own, raw_sib, raw_x, raw_xs)[slot], (f,)), preferred_element_type=F32)
-        for j in range(chans // 16):
+    def normalize(slot, f, hid, runs=all_runs):
+        place = slot % 2 + (1 - 2 * (slot % 2)) * (c % 2)
+        raw = (raw_own, raw_sib, raw_x, raw_xs)[slot]
+        y = jnp.dot(swap[...], tiles_of(raw, (f,), runs), preferred_element_type=F32)
+        for i, j in enumerate(runs):
             here = slice(16 * j, 16 * (j + 1))
             a, b = ab[slot, 0, f, here, :], ab[slot, 1, f, here, :]
             for h in range(rows):
-                z = y[h * 16 : (h + 1) * 16, j * cols : (j + 1) * cols] * a + b
+                z = y[h * 16 : (h + 1) * 16, i * cols : (i + 1) * cols] * a + b
                 z = z + z * jnp.tanh(z)
                 left = jnp.where(lane_t == 0, 0.0, pltpu.roll(z, 1, 1))
                 right = jnp.where(lane_t == cols - 1, 0.0, pltpu.roll(z, cols - 1, 1))
@@ -259,16 +310,17 @@
                 part = res[dt * chans : (dt + 1) * chans, j * cols : (j + 1) * cols]
                 acc[f + 2 - dt, first_row + j] += part * m
 
-    def stage(conv, norm):
+    def stage(conv, norms):
         n = rows // 2
-
         for p in range(2):
             if conv is not None:
                 q, f = conv
                 convolve(q + (1 - 2 * q) * (c // 2), f, hid_of[conv], p * n, n)
-            if norm is not None:
-                q, f = norm
-                normalize(2 * q + p, f, hid_of[norm], p + (1 - 2 * p) * (c % 2))
+            for slot, f, runs in norms[p]:
+                normalize(slot, f, hid_of[slot // 2, f], runs)
+
+    def both(q, f):
+        return [(2 * q, f, all_runs)], [(2 * q + 1, f, all_runs)]
 
     def finish(f):
         pieces = []
@@ -278,89 +330,116 @@
             pieces.append(value.astype(BF16).reshape(256, cols))
         y = jnp.dot(swap[...], jnp.concatenate(pieces, axis=1), preferred_element_type=F32).astype(BF16)
         for j in range(chans // 16):
-            obuf[f, 16 * j : 16 * (j + 1)] = y[:, j * cols : (j + 1) * cols].reshape(16, rows, cols)
-        out_copy(f).start()
-
-    def arrived(f):
-        for k in (2 * f, 2 * f + 1):
-            to_x(k).wait_recv()
-            forward(k).start()
-
-    def forwarded(f):
-        for k in (2 * f, 2 * f + 1):
-            forward(k).wait_recv()
+            out[f, 16 * j : 16 * (j + 1)] = y[:, j * cols : (j + 1) * cols].reshape(16, rows, cols)
+
+    def arrived(k):
+        to_x(k).wait_recv()
+        forward(k).start()
 
     def send_halo(i):
         @pl.when(t < tiles - 1)
         def _():
             pout[i] = acc[frames + i].astype(BF16)
+
+        @pl.when((t < tiles - 1) & (t != cross))
+        def _():
             send_part(i).start()
+
+        @pl.when(t == cross)
+        def _():
+            for j in range(RELAYS):
+                to_relay(i, j).start()
+
+    def relay_halo(i):
+        @pl.when(is_relay)
+        def _():
+            to_relay(i, 0).wait_recv()
+            from_relay(i, my_share).start()
+
+    def take_halo(i):
+        @pl.when((t > 0) & (t != cross + 1))
+        def _():
+            send_part(i).wait_recv()
+
+        @pl.when(t == cross + 1)
+        def _():
+            for j in range(RELAYS):
+                from_relay(i, j).wait_recv()
+
+        @pl.when(t > 0)
+        def _():
+            acc[i] += pin[i].astype(F32)
 
     own, rem = 0, 1
     steps = [(own, 3), (own, 2), (rem, 3), (own, 1), (rem, 2), (own, 0), (rem, 1), (rem, 0)]
     hid_of = {step: (hid_a, hid_b)[i % 2] for i, step in enumerate(steps)}
 
+    low, high = all_runs[: len(all_runs) // 2], all_runs[len(all_runs) // 2 :]
+    none = [], []
     send_ab(1).wait_recv()
     expand(1)
     for f in range(frames):
         to_sibling(f).wait_recv()
-    with jax.named_scope("norm_first"):
-        stage(None, (own, 3))
-    with jax.named_scope("own3"):
-        stage((own, 3), (own, 2))
-    arrived(3)
+    stage(None, both(own, 3))
+    arrived(6)
+    stage((own, 3), both(own, 2))
+    arrived(7)
     send_ab(2).wait_recv()
     expand(2)
     send_ab(3).wait_recv()
     expand(3)
-    forwarded(3)
-    with jax.named_scope("own2"):
-        stage((own, 2), (rem, 3))
-    with jax.named_scope("rem3"):
-        stage((rem, 3), (own, 1))
+    for k in (6, 7):
+        forward(k).wait_recv()
+    stage((own, 2), both(rem, 3))
+    arrived(4)
+    stage((rem, 3), both(own, 1))
     send_halo(1)
-    with jax.named_scope("wait2"):
-        arrived(2)
-        forwarded(2)
-    with jax.named_scope("own1"):
-        stage((own, 1), (rem, 2))
-    with jax.named_scope("rem2"):
-        stage((rem, 2), (own, 0))
+    to_x(order[6]).start()
+    arrived(5)
+    for k in (4, 5):
+        forward(k).wait_recv()
+    stage((own, 1), both(rem, 2))
+    stage((rem, 2), both(own, 0))
     send_halo(0)
-    with jax.named_scope("wait1"):
-        arrived(1)
-        forwarded(1)
-    with jax.named_scope("own0"):
-        stage((own, 0), (rem, 1))
-    with jax.named_scope("rem1"):
-        stage((rem, 1), None)
+    relay_halo(1)
+    to_x(order[7]).start()
+    arrived(2)
+    arrived(3)
+    for k in (2, 3):
+        forward(k).wait_recv()
+    stage((own, 0), both(rem, 1))
+    arrived(0)
+    stage((rem, 1), ([(2, 0, low)], []))
+    arrived(1)
+    relay_halo(0)
     finish(3)
-    with jax.named_scope("wait0"):
-        arrived(0)
-        forwarded(0)
-    with jax.named_scope("norm_last"):
-        stage(None, (rem, 0))
-    with jax.named_scope("rem0"):
-        stage((rem, 0), None)
-    with jax.named_scope("finish"):
-        finish(2)
-        for i in range(2):
-
-            @pl.when(t > 0)
-            def _():
-                send_part(1 - i).wait_recv()
-                acc[1 - i] += pin[1 - i].astype(F32)
-
-            finish(1 - i)
+    forward(0).wait_recv()
+    stage(None, ([(3, 0, low)], [(2, 0, high)]))
+    forward(1).wait_recv()
+    stage(None, ([(3, 0, high)], []))
+    stage((rem, 0), none)
+    finish(2)
+    take_halo(1)
+    finish(1)
+    take_halo(0)
+    finish(0)
 
     for i in range(2):
 
-        @pl.when(t < tiles - 1)
+        @pl.when((t < tiles - 1) & (t != cross))
         def _():
             send_part(i).wait_send()
 
-    for f in range(frames):
-        out_copy(f).wait()
+        @pl.when(t == cross)
+        def _():
+            for j in range(RELAYS):
+                to_relay(i, j).wait_send()
+
+        @pl.when(is_relay)
+        def _():
+            from_relay(i, my_share).wait_send()
+
+    for f in range(frames):
         to_sibling(f).wait_send()
     for k in order:
         to_x(k).wait_send()
@@ -381,12 +460,12 @@
     all_chans = conv_weight.shape[3]
     weight = jnp.swapaxes(conv_weight, 3, 4).reshape(3, 9, chans, all_chans)
     dma = pltpu.SemaphoreType.DMA
-    smem, anyspace = pl.BlockSpec(memory_space=pltpu.SMEM), pl.BlockSpec(memory_space=pl.ANY)
+    anyspace = pl.BlockSpec(memory_space=pltpu.HBM)
     return pl.pallas_call(
         kernel,
         out_shape=jax.ShapeDtypeStruct(video.shape, BF16),
-        in_specs=[smem] * 4 + [anyspace] * 2,
-        out_specs=anyspace,
+        in_specs=[anyspace] * 6,
+        out_specs=pl.BlockSpec(memory_space=pltpu.VMEM),
         scratch_shapes=[
             pltpu.VMEM((frames, chans, rows, cols), BF16),
             pltpu.VMEM((frames, chans, rows, cols), BF16),
@@ -399,7 +478,7 @@
             pltpu.VMEM((frames + 2, rows, chans, cols), F32),
             pltpu.VMEM((2, rows, chans, cols), BF16),
             pltpu.VMEM((2, rows, chans, cols), BF16),
-            pltpu.VMEM((frames, chans, rows, cols), BF16),
+            pltpu.VMEM((2, rows // RELAYS, chans, cols), BF16),
             pltpu.VMEM((4, 2, frames, chans, cols), F32),
             pltpu.VMEM((4, chans, cols), F32),
             pltpu.VMEM((3, chans, cols), F32),
@@ -408,12 +487,18 @@
             pltpu.VMEM((frames * groups, cols), F32),
             pltpu.VMEM((9, groups, cols), F32),
             pltpu.SMEM((3 * frames,), F32),
-            dma((frames,)), dma((3,)), dma((frames,)),
+            pltpu.SMEM(clip_lengths.shape, jnp.int32),
+            pltpu.SMEM((chans,), F32),
+            pltpu.SMEM((chans,), F32),
+            pltpu.SMEM((chans,), F32),
+            dma((4,)),
+            dma((frames,)), dma((3,)),
             dma((2 * frames,)), dma((2 * frames,)), dma((frames,)), dma((frames,)), dma((2 * frames,)), dma((2 * frames,)),
             dma((8,)), dma((8,)), dma((4,)), dma((4,)), dma((2,)), dma((2,)),
+            dma((2, RELAYS)), dma((2,)), dma((2,)), dma((2, RELAYS)),
         ],
         compiler_params=pltpu.CompilerParams(
-            collective_id=0, has_side_effects=True, vmem_limit_bytes=60 << 20
+            collective_id=0, has_side_effects=True, vmem_limit_bytes=58 << 20
         ),
         name="resblock",
     )(clip_lengths, norm_gain, norm_shift, conv_bias, video, weight)

time: 74.1 us -> 59.3 us (0.80)
  Pallas kernels: 71.1 us -> 56 us
    pallas_call x1, Pallas kernels: 71.1 us -> 56 us  [on_device(): pl.pallas_call(kernel, out_shape=jax.ShapeDtypeStruct(video.shape, BF16),...]
where the time goes in v2:
time: 59.3 us; the launch traced here: 58.9 us
  Pallas kernels  56 us (94%)
  local copies, waits for them, and re-layouts  2.82 us (5%)
    pallas_call x1, Pallas kernels, on_device(): pl.pallas_call(kernel, out_shape=jax.ShapeDtypeStruct(video.shape, BF16),...  56 us
    unnamed x1, local copies, waits for them, and re-layouts  2.82 us

profile of v2, /device:TPU:6, one launch (start us, length us, event | category | flops | bytes accessed | tf_op | source)
XLA Modules:
  0.0 58.9 jit_solution(797384871762726881)
XLA Ops:
  0.0 56.0 %resblock.1 = bf16[4,96,16,128]{3,2,1,0:T(8,128)(2,1)} custom-call(s32[32]{0:T(128)} %lens_in.1, f32[96]{0:T(128)} %gain_in.1, f32[96]{0:T(128)} %shift_in.1, f32[96]{0:T(128)} %bias_in.1, bf16[4,96,16,128]{3,2,1,0:T(8,128)(2,1)} %video.1, bf16[3,9,96,384]{3,2,1,0:T(8,128)(2,1)} %bitcast.3), custom_call_target="tpu_custom_call" | custom-call | tf_op jit(solution)/shard_map/resblock/pallas_call | solution.py:464
  56.0 2.8 %copy.8 = bf16[4,96,16,128]{3,2,1,0:T(8,128)(2,1)} copy(bf16[4,96,16,128]{3,2,1,0:T(8,128)(2,1)} %resblock.1) | data formatting | bytes 3145728

commit v3 on v2

--- a/solution.py
+++ b/solution.py
@@ -68,14 +68,12 @@
         return remote(pout.at[i], pin.at[i], ps.at[i], pr.at[i], (lax.rem(t + 1, tiles), c))
 
     cross = tiles // 2 - 1
-    first_relay = cross - 10
-    from_first = t - first_relay
-    is_relay = (from_first >= 0) & (from_first < 10) & ((from_first + tiles) % 4 < 3)
-    my_share = from_first - from_first // 4
+    is_relay = ((t % 2 == 1) & (t < cross)) | (t == cross - 1)
+    my_share = t // 2
     share = rows // RELAYS
 
     def relay(j):
-        return (first_relay + 4 * (j // 3) + j % 3, c)
+        return (2 * j + 1 if j < RELAYS - 1 else cross - 1, c)
 
     def to_relay(i, j):
         src = pout.at[i, pl.ds(j * share, share)]
@@ -498,7 +496,7 @@
             dma((2, RELAYS)), dma((2,)), dma((2,)), dma((2, RELAYS)),
         ],
         compiler_params=pltpu.CompilerParams(
-            collective_id=0, has_side_effects=True, vmem_limit_bytes=58 << 20
+            collective_id=0, has_side_effects=True, vmem_limit_bytes=52 << 20
         ),
         name="resblock",
     )(clip_lengths, norm_gain, norm_shift, conv_bias, video, weight)

time: 59.3 us -> 56.8 us (0.958)
  Pallas kernels: 56 us -> 52.8 us
  local copies, waits for them, and re-layouts: 2.82 us -> 3.76 us
    pallas_call x1, Pallas kernels: 56 us -> 52.8 us  [on_device(): pl.pallas_call(kernel, out_shape=jax.ShapeDtypeStruct(video.shape, BF16),...]
    unnamed x1 -> x9, local copies, waits for them, and re-layouts: 2.82 us -> 3.76 us
where the time goes in v3:
time: 56.8 us; the launch traced here: 56.6 us
  Pallas kernels  52.8 us (93%)
  local copies, waits for them, and re-layouts  3.76 us (7%)
    pallas_call x1, Pallas kernels, on_device(): pl.pallas_call(kernel, out_shape=jax.ShapeDtypeStruct(video.shape, BF16),...  52.8 us
    unnamed x9, local copies, waits for them, and re-layouts  3.76 us

profile of v3, /device:TPU:6, one launch (start us, length us, event | category | flops | bytes accessed | tf_op | source)
XLA Modules:
  0.0 56.6 jit_solution(5532276793652016787)
XLA Ops:
  0.0 0.0 copy-start
  0.0 0.7 %copy-done = s32[32]{0:T(128)S(1)} copy-done((s32[32]{0:T(128)S(1)}, s32[32]{0:T(128)}, u32[]{:S(2)}) %copy-start) | copy-done | bytes 152
  0.7 0.0 copy-start.1
  0.7 0.7 %copy-done.1 = f32[96]{0:T(128)S(1)} copy-done((f32[96]{0:T(128)S(1)}, f32[96]{0:T(128)}, u32[]{:S(2)}) %copy-start.1) | copy-done | bytes 408
  1.3 0.0 copy-start.2
  1.3 0.7 %copy-done.2 = f32[96]{0:T(128)S(1)} copy-done((f32[96]{0:T(128)S(1)}, f32[96]{0:T(128)}, u32[]{:S(2)}) %copy-start.2) | copy-done | bytes 408
  2.0 0.0 copy-start.3
  2.0 0.7 %copy-done.3 = f32[96]{0:T(128)S(1)} copy-done((f32[96]{0:T(128)S(1)}, f32[96]{0:T(128)}, u32[]{:S(2)}) %copy-start.3) | copy-done | bytes 408
  2.6 52.8 %resblock.1 = bf16[4,96,16,128]{3,2,1,0:T(8,128)(2,1)S(1)} custom-call(s32[32]{0:T(128)S(1)} %copy-done, f32[96]{0:T(128)S(1)} %copy-done.1, f32[96]{0:T(128)S(1)} %copy-done.2, f32[96]{0:T(128)S(1)} %copy-done.3, bf16[4,96,16,128]{3,2,1,0:T(8,128)(2,1)} %video.1, bf16[3,9,96,384]{3,2,1,0:T(8,128)(2,1)} %bitcast.3), custom_call_target="tpu_custom_call" | custom-call | tf_op jit(solution)/shard_map/resblock/pallas_call | solution.py:462
  55.5 1.1 %copy.8 = bf16[4,96,16,128]{3,2,1,0:T(8,128)(2,1)} copy(bf16[4,96,16,128]{3,2,1,0:T(8,128)(2,1)S(1)} %resblock.1) | data formatting | bytes 3145728
Async XLA Ops:
  0.0 0.7 %copy-start = (s32[32]{0:T(128)S(1)}, s32[32]{0:T(128)}, u32[]{:S(2)}) copy-start(s32[32]{0:T(128)} %lens_in.1) | copy-start | bytes 388
  0.7 0.7 %copy-start.1 = (f32[96]{0:T(128)S(1)}, f32[96]{0:T(128)}, u32[]{:S(2)}) copy-start(f32[96]{0:T(128)} %gain_in.1) | copy-start | bytes 1156
  1.3 0.7 %copy-start.2 = (f32[96]{0:T(128)S(1)}, f32[96]{0:T(128)}, u32[]{:S(2)}) copy-start(f32[96]{0:T(128)} %shift_in.1) | copy-start | bytes 1156
  2.0 0.7 %copy-start.3 = (f32[96]{0:T(128)S(1)}, f32[96]{0:T(128)}, u32[]{:S(2)}) copy-start(f32[96]{0:T(128)} %bias_in.1) | copy-start | bytes 1156
